TPU v7x, 32 devices: a whole 2x2x4 slice. The times are simulated.
32 devices in a mesh: dp: 4 (over y, core), ctx: 8 (over z, x).
Axes of the slice: x: 2, y: 2, z: 4, core: 2. Of those that a mesh axis runs over, the one named last changes fastest.
Arguments:
- queries: bfloat16 [4, 2048, 2560], P('dp', 'ctx'), may hold values from -120 to 120
- global_keys: bfloat16 [4, 2048, 512], P('dp', 'ctx'), may hold values from -5 to 5
- global_values: bfloat16 [4, 2048, 512], P('dp', 'ctx'), may hold values from -6 to 6
- out_grad: bfloat16 [4, 2048, 2560], P('dp', 'ctx'), may hold values from -6 to 6
- query_gain: float32 [2560], replicated, may hold values from 0.5 to 1.5
- doc_start: int32 [4, 16], P('dp', 'ctx'), may hold values from 0 to 15, as said below
Outputs:
- attn_out: bfloat16 [4, 2048, 2560], P('dp', 'ctx')
- query_grad: bfloat16 [4, 2048, 2560], P('dp', 'ctx')
- key_grad: bfloat16 [4, 2048, 512], P('dp', 'ctx')
- value_grad: bfloat16 [4, 2048, 512], P('dp', 'ctx')
- gain_grad: float32 [2560], replicated
Inputs may be any that keep to these rules, and one draw needn't show every extreme that they name: doc_start[g, b] is the first block of block b's document: it is at most b and at least b - 6, never falls along b, and equals b where a document begins; every slab has a document of exactly 7 blocks.
All inputs are finite; a program needn't handle non-finite values.
Results may differ from a plain program's by a relative error of at most 0.017.
The roundings to bfloat16 on the way count: a program that leaves them out, or rounds other values in their place, can miss the bound.
Values may be sent and summed in bfloat16 or wider, within the bound.
A program may use at most 64 MiB of HBM per device.

v0:
```python
import math

import jax
import jax.numpy as jnp
from jax import lax
from jax.sharding import PartitionSpec as P

HD = 128
BLOCK = 128
REACH = 4


def shifted(value, axis, steps):
    count = lax.axis_size(axis)
    first, last = (max(0, -steps), min(count, count - steps))
    return lax.ppermute(value, axis, [(source, source + steps) for source in range(first, last)])


def head_group(inputs, allowed, factor):
    query_part, key_part, value_part, grad_part = inputs
    scores = (
        jnp.einsum("tgd,wd->gtw", query_part, key_part, preferred_element_type=jnp.float32) * factor
    )
    scores = jnp.where(allowed[None], scores, -jnp.inf)
    row_max = jnp.max(scores, axis=-1, keepdims=True)
    log_total = row_max + jnp.log(jnp.sum(jnp.exp(scores - row_max), axis=-1, keepdims=True))
    weights = jnp.exp(scores - log_total)
    weights_low = weights.astype(jnp.bfloat16)
    result = jnp.einsum(
        "gtw,wd->tgd", weights_low, value_part, preferred_element_type=jnp.float32
    ).astype(jnp.bfloat16)
    inner_sum = jnp.einsum("tgd,tgd->gt", grad_part, result, preferred_element_type=jnp.float32)
    dweights = jnp.einsum("tgd,wd->gtw", grad_part, value_part, preferred_element_type=jnp.float32)
    dscore_low = (weights * (dweights - inner_sum[..., None])).astype(jnp.bfloat16)
    dquery = (
        jnp.einsum("gtw,wd->tgd", dscore_low, key_part, preferred_element_type=jnp.float32) * factor
    )
    dkey = (
        jnp.einsum("gtw,tgd->wd", dscore_low, query_part, preferred_element_type=jnp.float32)
        * factor
    )
    dvalue = jnp.einsum("gtw,tgd->wd", weights_low, grad_part, preferred_element_type=jnp.float32)
    return (result, dquery, dkey, dvalue)


def local(queries, global_keys, global_values, out_grad, query_gain, doc_start):
    row_count = queries.shape[1]
    reach = REACH
    width = reach * row_count
    device = lax.axis_index("ctx")
    query_rows = queries[0]
    key_rows = global_keys[0]
    value_rows = global_values[0]
    grad_rows = out_grad[0]
    kv_count = key_rows.shape[1] // HD
    group_size = query_rows.shape[1] // (kv_count * HD)
    factor = 1.0 / math.sqrt(HD)
    scaled = (query_rows.astype(jnp.float32) * query_gain).astype(jnp.bfloat16)
    key_list = [key_rows]
    value_list = [value_rows]
    for distance in range(1, reach):
        far_keys, far_values = shifted((key_rows, value_rows), "ctx", distance)
        key_list.insert(0, far_keys)
        value_list.insert(0, far_values)
    window_keys = jnp.concatenate(key_list, axis=0)
    window_values = jnp.concatenate(value_list, axis=0)
    first_device = device - (reach - 1)
    query_pos = device * row_count + jnp.arange(row_count, dtype=jnp.int32)
    key_pos = first_device * row_count + jnp.arange(width, dtype=jnp.int32)
    begins = jnp.repeat(doc_start[0], BLOCK) * BLOCK
    allowed = (key_pos[None, :] <= query_pos[:, None]) & (key_pos[None, :] >= begins[:, None])
    query_four = scaled.reshape(row_count, kv_count, group_size, HD).transpose(1, 0, 2, 3)
    grad_four = grad_rows.reshape(row_count, kv_count, group_size, HD).transpose(1, 0, 2, 3)
    key_three = window_keys.reshape(width, kv_count, HD).transpose(1, 0, 2)
    value_three = window_values.reshape(width, kv_count, HD).transpose(1, 0, 2)
    results, dqueries, dkeys, dvalues = lax.map(
        lambda inputs: head_group(inputs, allowed, factor),
        (query_four, key_three, value_three, grad_four),
    )
    attn_out = results.transpose(1, 0, 2, 3).reshape(row_count, -1)
    dscaled = dqueries.transpose(1, 0, 2, 3).reshape(row_count, -1)

    def by_offset(partial_value):
        return partial_value.reshape(kv_count, reach, row_count, HD)[:, ::-1]

    key_offsets = by_offset(dkeys)
    value_offsets = by_offset(dvalues)
    for bit_index in range(reach.bit_length() - 1):
        stride = 1 << bit_index
        got_keys, got_values = shifted(
            (key_offsets[:, 1::2], value_offsets[:, 1::2]), "ctx", -stride
        )
        key_offsets = key_offsets[:, 0::2] + got_keys
        value_offsets = value_offsets[:, 0::2] + got_values
    key_total = key_offsets[:, 0]
    value_total = value_offsets[:, 0]
    key_grad = key_total.transpose(1, 0, 2).reshape(row_count, -1).astype(jnp.bfloat16)
    value_grad = value_total.transpose(1, 0, 2).reshape(row_count, -1).astype(jnp.bfloat16)
    query_grad = (dscaled * query_gain).astype(jnp.bfloat16)
    gain_term = jnp.sum(dscaled * query_rows.astype(jnp.float32), axis=0)
    gain_grad = lax.psum(gain_term, ("dp", "ctx"))
    return (attn_out[None], query_grad[None], key_grad[None], value_grad[None], gain_grad)


def solution(mesh):
    return jax.shard_map(
        local,
        mesh=mesh,
        in_specs=(
            P("dp", "ctx", None),
            P("dp", "ctx", None),
            P("dp", "ctx", None),
            P("dp", "ctx", None),
            P(),
            P("dp", "ctx"),
        ),
        out_specs=(
            P("dp", "ctx", None),
            P("dp", "ctx", None),
            P("dp", "ctx", None),
            P("dp", "ctx", None),
            P(),
        ),
        check_vma=False,
    )
```

profile of v0, /device:TPU:0, one launch (start us, length us, event | category | flops | bytes accessed | tf_op | source)
XLA Modules:
  0.0 233.0 jit_solution(11764065059907299993)
XLA Ops:
  1.7 5.5 %collective-permute-start.5 = (bf16[256,512]{0,1:T(8,128)(2,1)S(1)}, bf16[256,512]{0,1:T(8,128)(2,1)}, u32[]{:S(2)}, u32[]{:S(2)}) collective-permute-start(bf16[256,512]{0,1:T(8,128)(2,1)S(1)} %bitcast.189), channel_id=1, source_target_pairs={{0,1},{1,2},{2,3},{3,4},{4,5},{5,6},{6,7},{8,9},{9,10},{10,11},{11... | collective-permute-start | bytes 786440 | tf_op jit(solution)/shard_map/ppermute | solution.py:16
  7.3 3.5 %collective-permute-start.4 = (bf16[256,512]{0,1:T(8,128)(2,1)S(1)}, bf16[256,512]{0,1:T(8,128)(2,1)}, u32[]{:S(2)}, u32[]{:S(2)}) collective-permute-start(bf16[256,512]{0,1:T(8,128)(2,1)S(1)} %bitcast.190), channel_id=1, source_target_pairs={{0,2},{1,3},{2,4},{3,5},{4,6},{5,7},{8,10},{9,11},{10,12},{11,13},... | collective-permute-start | bytes 786440 | tf_op jit(solution)/shard_map/ppermute | solution.py:16
  10.8 4.5 %collective-permute-start.3 = (bf16[256,512]{0,1:T(8,128)(2,1)S(1)}, bf16[256,512]{0,1:T(8,128)(2,1)}, u32[]{:S(2)}, u32[]{:S(2)}) collective-permute-start(bf16[256,512]{0,1:T(8,128)(2,1)S(1)} %bitcast.191), channel_id=1, source_target_pairs={{0,3},{1,4},{2,5},{3,6},{4,7},{8,11},{9,12},{10,13},{11,14},{12,15... | collective-permute-start | bytes 786440 | tf_op jit(solution)/shard_map/ppermute | solution.py:16
  15.3 3.4 %collective-permute-start.2 = (bf16[256,512]{1,0:T(8,128)(2,1)}, bf16[256,512]{1,0:T(8,128)(2,1)S(1)}, u32[]{:S(2)}, u32[]{:S(2)}) collective-permute-start(bf16[256,512]{1,0:T(8,128)(2,1)} %bitcast.197), channel_id=1, source_target_pairs={{0,1},{1,2},{2,3},{3,4},{4,5},{5,6},{6,7},{8,9},{9,10},{10,11},{11... | collective-permute-start | bytes 786440 | tf_op jit(solution)/shard_map/ppermute | solution.py:16
  18.7 2.0 collective-permute-start.1
  24.8 16.2 %collective-permute-start = (bf16[256,512]{1,0:T(8,128)(2,1)S(1)}, bf16[256,512]{1,0:T(8,128)(2,1)}, u32[]{:S(2)}, u32[]{:S(2)}) collective-permute-start(bf16[256,512]{1,0:T(8,128)(2,1)S(1)} %bitcast.199), channel_id=1, source_target_pairs={{0,3},{1,4},{2,5},{3,6},{4,7},{8,11},{9,12},{10,13},{11,14},{12,15... | collective-permute-start | bytes 786440 | tf_op jit(solution)/shard_map/ppermute | solution.py:16
  41.3 2.5 %copy.38 = bf16[1,256,2560]{1,2,0:T(8,128)(2,1)} copy(bf16[1,256,2560]{2,1,0:T(8,128)(2,1)} %param.11) | data formatting | bytes 2621440 | tf_op args[3]
  46.1 2.2 maximum_bitcast_fusion.1
  50.5 68.1 %while.17 = (s32[]{:T(128)}, bf16[4,256,5,128]{1,3,2,0:T(8,128)(2,1)}, f32[4,256,5,128]{1,3,2,0:T(8,128)}, f32[4,1024,128]{2,1,0:T(8,128)}, f32[4,1024,128]{2,1,...) while((s32[]{:T(128)}, ...), condition=%wide.region_3.4_spmd.clone, body=%wide.region_0.3_spmd.clone.sunk | while | flops 2042689024 | bytes 49229988 | solution.py:76
  52.3 2.0 fusion.65
  55.5 2.2 bitcast_dynamic-update-slice_fusion.2
  57.8 3.1 %fusion.69 = f32[4,1024,128]{2,1,0:T(8,128)} fusion(f32[4,1024,128]{2,1,0:T(8,128)} %get-tuple-element.252, s32[]{:T(128)S(6)} %copy.80, f32[1024,256,5]{1,0,2:T(8,128)S(1)} %get-tuple-element.231, f32[5,256]{1,0:T(8,128)S(1)} %log_add_fusion.2, pred[256,1024]{0,1:T(8,128)(4,1)S(1)} %compare_and_fusion.2, ...), kind=kOutput, calls=%fused_computation.13.clone.1 | convolution fusion | flops 340787200 | bytes 6363136 | tf_op jit(solution)/shard_map/while/body/eval_jaxpr/gtw,tgd->wd/dot_general | solution.py:42
  60.9 2.6 %fusion.66 = bf16[5,256,1024]{1,2,0:T(8,128)(2,1)S(1)} fusion(f32[1024,256,5]{1,0,2:T(8,128)S(1)} %get-tuple-element.231, f32[5,256]{1,0:T(8,128)S(1)} %multiply_reduce_fusion.2, f32[5,256]{1,0:T(8,128)S(1)} %log_add_fusion.2, pred[256,1024]{0,1:T(8,128)(4,1)S(1)} %compare_and_fusion.2, bf16[4,1024,128]{1,2,0:T(8,128)(2,1)S(1)} %copy-done.12, ...), kind=kOutput, calls=%fused_computation.3.clone.1 | convolution fusion | flops 343408640 | bytes 8733696 | tf_op jit(solution)/shard_map/while/body/eval_jaxpr/tgd,wd->gtw/dot_general | solution.py:33
  65.2 2.3 fusion.67
  69.3 2.0 fusion.65
  72.5 2.2 bitcast_dynamic-update-slice_fusion.2
  74.8 3.2 %fusion.69 = f32[4,1024,128]{2,1,0:T(8,128)} fusion(f32[4,1024,128]{2,1,0:T(8,128)} %get-tuple-element.252, s32[]{:T(128)S(6)} %copy.80, f32[1024,256,5]{1,0,2:T(8,128)S(1)} %get-tuple-element.231, f32[5,256]{1,0:T(8,128)S(1)} %log_add_fusion.2, pred[256,1024]{0,1:T(8,128)(4,1)S(1)} %compare_and_fusion.2, ...), kind=kOutput, calls=%fused_computation.13.clone.1 | convolution fusion | flops 340787200 | bytes 6363136 | tf_op jit(solution)/shard_map/while/body/eval_jaxpr/gtw,tgd->wd/dot_general | solution.py:42
  78.0 2.6 %fusion.66 = bf16[5,256,1024]{1,2,0:T(8,128)(2,1)S(1)} fusion(f32[1024,256,5]{1,0,2:T(8,128)S(1)} %get-tuple-element.231, f32[5,256]{1,0:T(8,128)S(1)} %multiply_reduce_fusion.2, f32[5,256]{1,0:T(8,128)S(1)} %log_add_fusion.2, pred[256,1024]{0,1:T(8,128)(4,1)S(1)} %compare_and_fusion.2, bf16[4,1024,128]{1,2,0:T(8,128)(2,1)S(1)} %copy-done.12, ...), kind=kOutput, calls=%fused_computation.3.clone.1 | convolution fusion | flops 343408640 | bytes 8733696 | tf_op jit(solution)/shard_map/while/body/eval_jaxpr/tgd,wd->gtw/dot_general | solution.py:33
  82.3 2.3 fusion.67
  89.6 2.2 bitcast_dynamic-update-slice_fusion.2
  91.9 3.1 %fusion.69 = f32[4,1024,128]{2,1,0:T(8,128)} fusion(f32[4,1024,128]{2,1,0:T(8,128)} %get-tuple-element.252, s32[]{:T(128)S(6)} %copy.80, f32[1024,256,5]{1,0,2:T(8,128)S(1)} %get-tuple-element.231, f32[5,256]{1,0:T(8,128)S(1)} %log_add_fusion.2, pred[256,1024]{0,1:T(8,128)(4,1)S(1)} %compare_and_fusion.2, ...), kind=kOutput, calls=%fused_computation.13.clone.1 | convolution fusion | flops 340787200 | bytes 6363136 | tf_op jit(solution)/shard_map/while/body/eval_jaxpr/gtw,tgd->wd/dot_general | solution.py:42
  95.0 2.6 %fusion.66 = bf16[5,256,1024]{1,2,0:T(8,128)(2,1)S(1)} fusion(f32[1024,256,5]{1,0,2:T(8,128)S(1)} %get-tuple-element.231, f32[5,256]{1,0:T(8,128)S(1)} %multiply_reduce_fusion.2, f32[5,256]{1,0:T(8,128)S(1)} %log_add_fusion.2, pred[256,1024]{0,1:T(8,128)(4,1)S(1)} %compare_and_fusion.2, bf16[4,1024,128]{1,2,0:T(8,128)(2,1)S(1)} %copy-done.12, ...), kind=kOutput, calls=%fused_computation.3.clone.1 | convolution fusion | flops 343408640 | bytes 8733696 | tf_op jit(solution)/shard_map/while/body/eval_jaxpr/tgd,wd->gtw/dot_general | solution.py:33
  99.3 2.3 fusion.67
  106.6 2.2 bitcast_dynamic-update-slice_fusion.2
  108.9 3.1 %fusion.69 = f32[4,1024,128]{2,1,0:T(8,128)} fusion(f32[4,1024,128]{2,1,0:T(8,128)} %get-tuple-element.252, s32[]{:T(128)S(6)} %copy.80, f32[1024,256,5]{1,0,2:T(8,128)S(1)} %get-tuple-element.231, f32[5,256]{1,0:T(8,128)S(1)} %log_add_fusion.2, pred[256,1024]{0,1:T(8,128)(4,1)S(1)} %compare_and_fusion.2, ...), kind=kOutput, calls=%fused_computation.13.clone.1 | convolution fusion | flops 340787200 | bytes 6363136 | tf_op jit(solution)/shard_map/while/body/eval_jaxpr/gtw,tgd->wd/dot_general | solution.py:42
  112.0 2.6 %fusion.66 = bf16[5,256,1024]{1,2,0:T(8,128)(2,1)S(1)} fusion(f32[1024,256,5]{1,0,2:T(8,128)S(1)} %get-tuple-element.231, f32[5,256]{1,0:T(8,128)S(1)} %multiply_reduce_fusion.2, f32[5,256]{1,0:T(8,128)S(1)} %log_add_fusion.2, pred[256,1024]{0,1:T(8,128)(4,1)S(1)} %compare_and_fusion.2, bf16[4,1024,128]{1,2,0:T(8,128)(2,1)S(1)} %copy-done.12, ...), kind=kOutput, calls=%fused_computation.3.clone.1 | convolution fusion | flops 343408640 | bytes 8733696 | tf_op jit(solution)/shard_map/while/body/eval_jaxpr/tgd,wd->gtw/dot_general | solution.py:33
  116.3 2.3 fusion.67
  128.7 2.3 slice.43
  133.9 19.4 %collective-permute-done.8 = f32[4,2,256,128]{3,0,2,1:T(4,128)} collective-permute-done((f32[4,2,256,128]{3,0,2,1:T(4,128)}, f32[4,2,256,128]{3,0,2,1:T(4,128)}, u32[]{:S(2)}, u32[]{:S(2)}) %collective-permute-start.8) | collective-permute-done | bytes 1048608 | tf_op jit(solution)/shard_map/ppermute | solution.py:16
  157.1 15.3 %collective-permute-done.6 = f32[4,2,256,128]{3,0,2,1:T(4,128)S(1)} collective-permute-done((f32[4,2,256,128]{3,0,2,1:T(4,128)}, f32[4,2,256,128]{3,0,2,1:T(4,128)S(1)}, u32[]{:S(2)}, u32[]{:S(2)}) %collective-permute-start.6) | collective-permute-done | bytes 1048608 | tf_op jit(solution)/shard_map/ppermute | solution.py:16
  176.4 2.6 %copy.46 = bf16[1,256,2560]{2,1,0:T(8,128)(2,1)} copy(bf16[1,256,2560]{1,2,0:T(8,128)(2,1)} %bitcast.188) | data formatting | bytes 2621440
  180.6 48.4 %psum.7 = f32[2560]{0:T(1024)} all-reduce(f32[2560]{0:T(1024)S(1)} %reduce_sum.21), channel_id=1, replica_groups=mesh['dp'=4,'ctx'=8] {'dp','ctx'}, use_global_device_ids=true, to_apply=%region_5.6 | all-reduce | flops 2560 | bytes 20480 | tf_op jit(solution)/shard_map/psum | solution.py:101
  (126 shorter events, 58.9 us)
Async XLA Ops:
  1.7 44.3 %collective-permute-start.5 = (bf16[256,512]{0,1:T(8,128)(2,1)S(1)}, bf16[256,512]{0,1:T(8,128)(2,1)}, u32[]{:S(2)}, u32[]{:S(2)}) collective-permute-start(bf16[256,512]{0,1:T(8,128)(2,1)S(1)} %bitcast.189), channel_id=1, source_target_pairs={{0,1},{1,2},{2,3},{3,4},{4,5},{5,6},{6,7},{8,9},{9,10},{10,11},{11... | collective-permute-start | bytes 786440 | tf_op jit(solution)/shard_map/ppermute | solution.py:16
  7.3 38.8 %collective-permute-start.4 = (bf16[256,512]{0,1:T(8,128)(2,1)S(1)}, bf16[256,512]{0,1:T(8,128)(2,1)}, u32[]{:S(2)}, u32[]{:S(2)}) collective-permute-start(bf16[256,512]{0,1:T(8,128)(2,1)S(1)} %bitcast.190), channel_id=1, source_target_pairs={{0,2},{1,3},{2,4},{3,5},{4,6},{5,7},{8,10},{9,11},{10,12},{11,13},... | collective-permute-start | bytes 786440 | tf_op jit(solution)/shard_map/ppermute | solution.py:16
  10.8 35.3 %collective-permute-start.3 = (bf16[256,512]{0,1:T(8,128)(2,1)S(1)}, bf16[256,512]{0,1:T(8,128)(2,1)}, u32[]{:S(2)}, u32[]{:S(2)}) collective-permute-start(bf16[256,512]{0,1:T(8,128)(2,1)S(1)} %bitcast.191), channel_id=1, source_target_pairs={{0,3},{1,4},{2,5},{3,6},{4,7},{8,11},{9,12},{10,13},{11,14},{12,15... | collective-permute-start | bytes 786440 | tf_op jit(solution)/shard_map/ppermute | solution.py:16
  15.3 9.6 %collective-permute-start.2 = (bf16[256,512]{1,0:T(8,128)(2,1)}, bf16[256,512]{1,0:T(8,128)(2,1)S(1)}, u32[]{:S(2)}, u32[]{:S(2)}) collective-permute-start(bf16[256,512]{1,0:T(8,128)(2,1)} %bitcast.197), channel_id=1, source_target_pairs={{0,1},{1,2},{2,3},{3,4},{4,5},{5,6},{6,7},{8,9},{9,10},{10,11},{11... | collective-permute-start | bytes 786440 | tf_op jit(solution)/shard_map/ppermute | solution.py:16
  18.7 26.2 %collective-permute-start.1 = (bf16[256,512]{1,0:T(8,128)(2,1)}, bf16[256,512]{1,0:T(8,128)(2,1)}, u32[]{:S(2)}, u32[]{:S(2)}) collective-permute-start(bf16[256,512]{1,0:T(8,128)(2,1)} %bitcast.198), channel_id=1, source_target_pairs={{0,2},{1,3},{2,4},{3,5},{4,6},{5,7},{8,10},{9,11},{10,12},{11,13},... | collective-permute-start | bytes 786440 | tf_op jit(solution)/shard_map/ppermute | solution.py:16
  23.0 20.7 %copy-start = (f32[1,256,2560]{1,2,0:T(8,128)}, f32[1,256,2560]{1,2,0:T(8,128)S(1)}, u32[]{:S(2)}) copy-start(f32[1,256,2560]{1,2,0:T(8,128)S(1)} %copy.37) | copy-start | bytes 7864324
  23.0 1.8 copy-start.16
  23.0 1.8 copy-start.13
  24.8 16.2 %copy-start.14 = (bf16[256,512]{1,0:T(8,128)(2,1)}, bf16[256,512]{1,0:T(8,128)(2,1)S(1)}, u32[]{:S(2)}) copy-start(bf16[256,512]{1,0:T(8,128)(2,1)S(1)} %collective-permute-done.2) | copy-start | bytes 786436
  24.8 23.4 %collective-permute-start = (bf16[256,512]{1,0:T(8,128)(2,1)S(1)}, bf16[256,512]{1,0:T(8,128)(2,1)}, u32[]{:S(2)}, u32[]{:S(2)}) collective-permute-start(bf16[256,512]{1,0:T(8,128)(2,1)S(1)} %bitcast.199), channel_id=1, source_target_pairs={{0,3},{1,4},{2,5},{3,6},{4,7},{8,11},{9,12},{10,13},{11,14},{12,15... | collective-permute-start | bytes 786440 | tf_op jit(solution)/shard_map/ppermute | solution.py:16
  44.8 5.7 %copy-start.2 = (bf16[4,256,5,128]{1,3,2,0:T(8,128)(2,1)S(1)}, bf16[4,256,5,128]{1,3,2,0:T(8,128)(2,1)}, u32[]{:S(2)}) copy-start(bf16[4,256,5,128]{1,3,2,0:T(8,128)(2,1)} %fusion.35) | copy-start | bytes 3932164
  54.3 1.2 copy-start.12
  71.3 1.2 copy-start.12
  88.3 1.2 copy-start.12
  105.4 1.2 copy-start.12
  122.0 3.2 %copy-start.11 = (f32[4,1024,128]{2,1,0:T(8,128)S(1)}, f32[4,1024,128]{2,1,0:T(8,128)}, u32[]{:S(2)}) copy-start(f32[4,1024,128]{2,1,0:T(8,128)} %get-tuple-element.62) | copy-start | bytes 6291460
  123.7 29.6 %collective-permute-start.8 = (f32[4,2,256,128]{3,0,2,1:T(4,128)}, f32[4,2,256,128]{3,0,2,1:T(4,128)}, u32[]{:S(2)}, u32[]{:S(2)}) collective-permute-start(f32[4,2,256,128]{3,0,2,1:T(4,128)} %slice.49), channel_id=1, source_target_pairs={{1,0},{2,1},{3,2},{4,3},{5,4},{6,5},{7,6},{9,8},{10,9},{11,10},{12... | collective-permute-start | bytes 3145736 | tf_op jit(solution)/shard_map/ppermute | solution.py:16
  127.1 5.4 %copy-start.3 = (f32[4,256,5,128]{1,3,2,0:T(8,128)S(1)}, f32[4,256,5,128]{1,3,2,0:T(8,128)}, u32[]{:S(2)}) copy-start(f32[4,256,5,128]{1,3,2,0:T(8,128)} %get-tuple-element.61) | copy-start | bytes 7864324
  127.1 5.4 %copy-start.15 = (f32[2560]{0:T(1024)S(1)}, f32[2560]{0:T(1024)}, u32[]{:S(2)}) copy-start(f32[2560]{0:T(1024)} %param.12) | copy-start | bytes 30724
  131.0 22.3 %copy-start.9 = (f32[4,2,256,128]{3,0,2,1:T(4,128)S(1)}, f32[4,2,256,128]{3,0,2,1:T(4,128)}, u32[]{:S(2)}) copy-start(f32[4,2,256,128]{3,0,2,1:T(4,128)} %copy.65) | copy-start | bytes 3145732
  131.0 41.4 %collective-permute-start.6 = (f32[4,2,256,128]{3,0,2,1:T(4,128)}, f32[4,2,256,128]{3,0,2,1:T(4,128)S(1)}, u32[]{:S(2)}, u32[]{:S(2)}) collective-permute-start(f32[4,2,256,128]{3,0,2,1:T(4,128)} %slice.43), channel_id=1, source_target_pairs={{1,0},{2,1},{3,2},{4,3},{5,4},{6,5},{7,6},{9,8},{10,9},{11,10},{12... | collective-permute-start | bytes 3145736 | tf_op jit(solution)/shard_map/ppermute | solution.py:16
  133.9 38.5 %copy-start.10 = (f32[4,2,256,128]{3,0,2,1:T(4,128)S(1)}, f32[4,2,256,128]{3,0,2,1:T(4,128)}, u32[]{:S(2)}) copy-start(f32[4,2,256,128]{3,0,2,1:T(4,128)} %copy.63) | copy-start | bytes 3145732
  154.8 19.8 %copy-start.5 = (f32[4,2,256,128]{3,0,2,1:T(4,128)}, f32[4,2,256,128]{3,0,2,1:T(4,128)S(1)}, u32[]{:S(2)}) copy-start(f32[4,2,256,128]{3,0,2,1:T(4,128)S(1)} %reverse_add_fusion) | copy-start | bytes 3145732
  154.8 21.1 %copy-start.1 = (f32[1,256,2560]{1,2,0:T(8,128)S(1)}, f32[1,256,2560]{1,2,0:T(8,128)}, u32[]{:S(2)}) copy-start(f32[1,256,2560]{1,2,0:T(8,128)} %copy-done) | copy-start | bytes 7864324
  155.7 73.3 %collective-permute-start.9 = (f32[4,1,256,128]{3,0,2,1:T(4,128)}, f32[4,1,256,128]{3,0,2,1:T(4,128)}, u32[]{:S(2)}, u32[]{:S(2)}) collective-permute-start(f32[4,1,256,128]{3,0,2,1:T(4,128)} %slice.55), channel_id=1, source_target_pairs={{2,0},{3,1},{4,2},{5,3},{6,4},{7,5},{10,8},{11,9},{12,10},{13,11},... | collective-permute-start | bytes 1572872 | tf_op jit(solution)/shard_map/ppermute | solution.py:16
  172.7 1.0 copy-start.7
  174.6 56.4 %collective-permute-start.7 = (f32[4,1,256,128]{3,0,2,1:T(4,128)}, f32[4,1,256,128]{3,0,2,1:T(4,128)}, u32[]{:S(2)}, u32[]{:S(2)}) collective-permute-start(f32[4,1,256,128]{3,0,2,1:T(4,128)} %slice.53), channel_id=1, source_target_pairs={{2,0},{3,1},{4,2},{5,3},{6,4},{7,5},{10,8},{11,9},{12,10},{13,11},... | collective-permute-start | bytes 1572872 | tf_op jit(solution)/shard_map/ppermute | solution.py:16
  176.4 2.6 %copy-start.4 = (bf16[1,256,2560]{1,2,0:T(8,128)(2,1)S(1)}, bf16[1,256,2560]{1,2,0:T(8,128)(2,1)}, u32[]{:S(2)}) copy-start(bf16[1,256,2560]{1,2,0:T(8,128)(2,1)} %multiply_convert_fusion) | copy-start | bytes 3932164
  176.4 52.6 %copy-start.6 = (f32[4,2,256,128]{3,0,2,1:T(4,128)S(1)}, f32[4,2,256,128]{3,0,2,1:T(4,128)}, u32[]{:S(2)}) copy-start(f32[4,2,256,128]{3,0,2,1:T(4,128)} %copy-done.5) | copy-start | bytes 3145732
  179.0 52.0 %copy-start.8 = (f32[4,2,256,128]{3,0,2,1:T(4,128)S(1)}, f32[4,2,256,128]{3,0,2,1:T(4,128)}, u32[]{:S(2)}) copy-start(f32[4,2,256,128]{3,0,2,1:T(4,128)} %copy-done.7) | copy-start | bytes 3145732
where the time goes:
time: 235 us; the launch traced here: 233 us
  matrix products  55.5 us (24%)
  blocking collectives  48.4 us (21%)
  starting transfers between devices  40.7 us (17%)
  local copies, waits for them, and re-layouts  35 us (15%)
  waiting for transfers between devices  34.7 us (15%)
  other arithmetic  17.3 us (7%)
    psum x1, blocking collectives, local(): gain_grad = lax.psum(gain_term, ('dp', 'ctx'))  48.4 us
    ppermute x10, starting transfers between devices, shifted(): lax.ppermute(value, axis, [(source, source + steps) for source in range(f...  40.7 us
    ppermute x10, waiting for transfers between devices, shifted(): lax.ppermute(value, axis, [(source, source + steps) for source in range(f...  34.7 us
    unnamed x41, local copies, waits for them, and re-layouts  14.6 us
    dot_general x4, matrix products, head_group(): jnp.einsum('gtw,tgd->wd', weights_low, grad_part, preferred_element_type=...  12.5 us
    dot_general x4, matrix products, head_group(): jnp.einsum('tgd,wd->gtw', grad_part, value_part, preferred_element_type=j...  10.4 us
    dot_general x4, matrix products, head_group(): jnp.einsum('gtw,wd->tgd', dscore_low, key_part, preferred_element_type=jn...  9.27 us
    dot_general x4, matrix products, head_group(): jnp.einsum('gtw,wd->tgd', weights_low, value_part, preferred_element_type...  8.8 us
  transfers between devices with their start and end apart: 10, of which 2 were waited for; matrix products, arithmetic and copies ran while one was open for 12% of the time, Pallas kernels for 0%

commit v1 on v0

v1 whole, which is shorter than its diff:
```python
import functools
import math

import jax
import jax.numpy as jnp
from jax import lax
from jax.experimental import pallas as pl
from jax.experimental.pallas import tpu as pltpu
from jax.sharding import PartitionSpec as P

HD = 128
BLOCK = 128
REACH = 4
FAR = REACH - 1
NEG = -1e30
MESH = pl.DeviceIdType.MESH


def nt(left, right):
    return lax.dot_general(left, right, (((1,), (1,)), ((), ())), preferred_element_type=jnp.float32)


def nn(left, right):
    return jnp.dot(left, right, preferred_element_type=jnp.float32)


def kernel(
    n_dp,
    n_ctx,
    q_hbm,
    k_hbm,
    v_hbm,
    g_hbm,
    gain_ref,
    begins_ref,
    out_hbm,
    dq_hbm,
    dk_hbm,
    dv_hbm,
    gain_out,
    q_buf,
    g_buf,
    kv_buf,
    tri,
    s_buf,
    dp_buf,
    p_all,
    ds_all,
    qs_all,
    k_t,
    v_t,
    part_out,
    part_in,
    part_own,
    out_buf,
    dq_buf,
    kv_out,
    term,
    term_ctx,
    total,
    total_dp,
    load_sem,
    own_sem,
    send_sem,
    recv_sem,
    psend_sem,
    precv_sem,
    store_sem,
    kvst_sem,
    csend_sem,
    crecv_sem,
    dsend_sem,
    drecv_sem,
):
    heads, rows, _ = q_buf.shape
    kv_count = kv_buf.shape[0]
    group = heads // kv_count
    width = REACH * rows
    dp = lax.axis_index("dp")
    me = lax.axis_index("ctx")
    factor = 1.0 / math.sqrt(HD)
    log2_factor = factor * math.log2(math.e)

    def cols(index):
        return pl.ds(pl.multiple_of(index * HD, HD), HD)

    def load_q(h):
        return pltpu.make_async_copy(q_hbm.at[0, :, cols(h)], q_buf.at[h], load_sem.at[0, h])

    def load_g(h):
        return pltpu.make_async_copy(g_hbm.at[0, :, cols(h)], g_buf.at[h], load_sem.at[1, h])

    def load_k(c):
        return pltpu.make_async_copy(k_hbm.at[0, :, cols(c)], kv_buf.at[c, 0, FAR], own_sem.at[0, c])

    def load_v(c):
        return pltpu.make_async_copy(v_hbm.at[0, :, cols(c)], kv_buf.at[c, 1, FAR], own_sem.at[1, c])

    def send_kv(c, dist, which):
        source = (k_hbm, v_hbm)[which]
        return pltpu.make_async_remote_copy(
            src_ref=source.at[0, :, cols(c)],
            dst_ref=kv_buf.at[c, which, FAR - dist],
            send_sem=send_sem.at[c, dist - 1, which],
            recv_sem=recv_sem.at[c, dist - 1, which],
            device_id={"ctx": lax.rem(me + dist, n_ctx)},
            device_id_type=MESH,
        )

    def send_part(c, dist):
        return pltpu.make_async_remote_copy(
            src_ref=part_out.at[c, dist - 1],
            dst_ref=part_in.at[c, dist - 1],
            send_sem=psend_sem.at[c, dist - 1],
            recv_sem=precv_sem.at[c, dist - 1],
            device_id={"ctx": lax.rem(me + n_ctx - dist, n_ctx)},
            device_id_type=MESH,
        )

    def store_out(h):
        return pltpu.make_async_copy(out_buf.at[h], out_hbm.at[0, :, cols(h)], store_sem.at[0, h])

    def store_dq(h):
        return pltpu.make_async_copy(dq_buf.at[h], dq_hbm.at[0, :, cols(h)], store_sem.at[1, h])

    def store_dk(c):
        return pltpu.make_async_copy(kv_out.at[c, 0], dk_hbm.at[0, :, cols(c)], kvst_sem.at[0, c])

    def store_dv(c):
        return pltpu.make_async_copy(kv_out.at[c, 1], dv_hbm.at[0, :, cols(c)], kvst_sem.at[1, c])

    def send_ctx(step):
        return pltpu.make_async_remote_copy(
            src_ref=term,
            dst_ref=term_ctx.at[me],
            send_sem=csend_sem.at[step],
            recv_sem=crecv_sem.at[me],
            device_id={"ctx": lax.rem(me + step, n_ctx)},
            device_id_type=MESH,
        )

    def recv_ctx(peer):
        return pltpu.make_async_remote_copy(
            src_ref=term,
            dst_ref=term_ctx.at[peer],
            send_sem=csend_sem.at[0],
            recv_sem=crecv_sem.at[peer],
            device_id={"ctx": peer},
            device_id_type=MESH,
        )

    def send_dp(step):
        return pltpu.make_async_remote_copy(
            src_ref=total,
            dst_ref=total_dp.at[dp],
            send_sem=dsend_sem.at[step],
            recv_sem=drecv_sem.at[dp],
            device_id={"dp": lax.rem(dp + step, n_dp)},
            device_id_type=MESH,
        )

    def recv_dp(peer):
        return pltpu.make_async_remote_copy(
            src_ref=total,
            dst_ref=total_dp.at[peer],
            send_sem=dsend_sem.at[0],
            recv_sem=drecv_sem.at[peer],
            device_id={"dp": peer},
            device_id_type=MESH,
        )

    def each(count, body, start=0):
        def step(i, carry):
            body(i)
            return carry

        lax.fori_loop(start, count, step, 0)

    barrier = pltpu.get_barrier_semaphore()

    def greet_ctx(step):
        pl.semaphore_signal(
            barrier, inc=1, device_id={"ctx": lax.rem(me + step, n_ctx)}, device_id_type=MESH
        )

    def greet_dp(step):
        pl.semaphore_signal(
            barrier, inc=1, device_id={"dp": lax.rem(dp + step, n_dp)}, device_id_type=MESH
        )

    each(n_ctx, greet_ctx, 1)
    each(n_dp, greet_dp, 1)

    def start_loads(c):
        load_k(c).start()
        load_v(c).start()
        each(group, lambda g: (load_q(c * group + g).start(), load_g(c * group + g).start()))

    each(kv_count, start_loads)

    for dist in range(1, REACH):

        @pl.when(me < dist)
        def _():
            kv_buf[:, :, FAR - dist] = jnp.zeros((kv_count, 2, rows, HD), jnp.bfloat16)

    query_pos = me * rows + lax.broadcasted_iota(jnp.int32, (1, rows), 1)
    begins = begins_ref[...]
    key_pos = me * rows + lax.broadcasted_iota(jnp.int32, (rows, rows), 0)
    tri[...] = jnp.where((key_pos <= query_pos) & (key_pos >= begins), 0.0, NEG)

    pl.semaphore_wait(barrier, n_ctx - 1 + n_dp - 1)

    def start_sends(c):
        for dist in range(1, REACH):

            @pl.when(me + dist < n_ctx)
            def _():
                send_kv(c, dist, 0).start()
                send_kv(c, dist, 1).start()

    each(kv_count, start_sends)

    far_blocks = FAR * rows // BLOCK
    shown = []
    for w in range(far_blocks):
        first = (me - FAR) * rows + w * BLOCK
        shown.append(begins <= first)

    def one_kv(c):
        load_k(c).wait()
        load_v(c).wait()
        for dist in range(1, REACH):

            @pl.when(me >= dist)
            def _():
                send_kv(c, dist, 0).wait_recv()
                send_kv(c, dist, 1).wait_recv()

        keys = kv_buf[c, 0].reshape(width, HD)
        values = kv_buf[c, 1].reshape(width, HD)
        k_t[...] = keys.astype(jnp.float32).T.astype(jnp.bfloat16)
        v_t[...] = values.astype(jnp.float32).T.astype(jnp.bfloat16)

        for g in range(group):
            h = c * group + g
            lanes = pl.ds(g * rows, rows)
            s_g = s_buf.at[g % 2]
            dp_g = dp_buf.at[g % 2]
            load_q(h).wait()
            load_g(h).wait()
            gain = gain_ref[pl.ds(h, 1), :]
            raw = q_buf[h].astype(jnp.float32)
            query = (raw * gain).astype(jnp.bfloat16)
            qs_all[lanes, :] = query
            grad = g_buf[h]
            s_g[...] = nt(kv_buf[c, 0].reshape(width, HD), query)
            dp_g[...] = nt(kv_buf[c, 1].reshape(width, HD), grad)
            near = s_g[FAR * rows :, :] + tri[...]
            s_g[FAR * rows :, :] = near
            top = jnp.max(near, axis=0, keepdims=True)
            for w in range(far_blocks):
                block_top = jnp.max(s_g[w * BLOCK : (w + 1) * BLOCK, :], axis=0, keepdims=True)
                top = jnp.maximum(top, jnp.where(shown[w], block_top, NEG))
            top = top * log2_factor
            norm = jnp.zeros((1, rows), jnp.float32)
            for w in range(width // BLOCK):
                at = slice(w * BLOCK, (w + 1) * BLOCK)
                shift = top if w >= far_blocks else jnp.where(shown[w], top, -NEG)
                prob = jnp.exp2(s_g[at, :] * log2_factor - shift)
                norm = norm + jnp.sum(prob, axis=0, keepdims=True)
                s_g[at, :] = prob
            inverse = 1.0 / norm
            for w in range(width // BLOCK):
                at = slice(w * BLOCK, (w + 1) * BLOCK)
                p_all[at, lanes] = (s_g[at, :] * inverse).astype(jnp.bfloat16)
            result_t = nn(v_t[...], p_all[:, lanes])
            out_buf[h] = result_t.T.astype(jnp.bfloat16)
            grad_t = grad.astype(jnp.float32).T
            rounded = result_t.astype(jnp.bfloat16).astype(jnp.float32)
            delta = jnp.sum(grad_t * rounded, axis=0, keepdims=True)
            store_out(h).start()
            for w in range(width // BLOCK):
                at = slice(w * BLOCK, (w + 1) * BLOCK)
                ds = (s_g[at, :] * inverse) * (dp_g[at, :] - delta)
                ds_all[at, lanes] = ds.astype(jnp.bfloat16)
            dscaled = (nn(k_t[...], ds_all[:, lanes]) * factor).T
            dq_buf[h] = (dscaled * gain).astype(jnp.bfloat16)
            store_dq(h).start()
            term[pl.ds(h, 1), :] = jnp.sum(dscaled * raw, axis=0, keepdims=True)

        all_grads = g_buf[pl.ds(c * group, group)].reshape(group * rows, HD)
        for dist in range(FAR, -1, -1):
            at = slice((FAR - dist) * rows, (FAR - dist + 1) * rows)
            dkey = nn(ds_all[at, :], qs_all[...]) * factor
            dvalue = nn(p_all[at, :], all_grads)
            if dist == 0:
                part_own[c, 0] = dkey
                part_own[c, 1] = dvalue
            else:
                part_out[c, dist - 1, 0] = dkey.astype(jnp.bfloat16)
                part_out[c, dist - 1, 1] = dvalue.astype(jnp.bfloat16)

                @pl.when(me >= dist)
                def _():
                    send_part(c, dist).start()

    each(kv_count, one_kv)

    each(n_ctx, lambda i: send_ctx(i).start(), 1)

    for dist in range(1, REACH):

        @pl.when(me + dist >= n_ctx)
        def _():
            part_in[:, dist - 1] = jnp.zeros((kv_count, 2, rows, HD), jnp.bfloat16)

    def finish_kv(c):
        for dist in range(1, REACH):

            @pl.when(me + dist < n_ctx)
            def _():
                send_part(c, dist).wait_recv()

        for which in range(2):
            whole = part_own[c, which]
            for dist in range(1, REACH):
                whole = whole + part_in[c, dist - 1, which].astype(jnp.float32)
            kv_out[c, which] = whole.astype(jnp.bfloat16)
        store_dk(c).start()
        store_dv(c).start()

    each(kv_count - 1, finish_kv)

    each(n_ctx, lambda i: recv_ctx(lax.rem(me + i, n_ctx)).wait_recv(), 1)
    term_ctx[me] = term[...]
    total[...] = lax.fori_loop(
        0, n_ctx, lambda i, carry: carry + term_ctx[i], jnp.zeros(total.shape, jnp.float32)
    )
    each(n_dp, lambda i: send_dp(i).start(), 1)

    finish_kv(kv_count - 1)

    each(n_dp, lambda i: recv_dp(lax.rem(dp + i, n_dp)).wait_recv(), 1)
    total_dp[dp] = total[...]
    gain_out[...] = lax.fori_loop(
        0, n_dp, lambda i, carry: carry + total_dp[i], jnp.zeros(total.shape, jnp.float32)
    )

    each(n_ctx, lambda i: send_ctx(i).wait_send(), 1)
    each(n_dp, lambda i: send_dp(i).wait_send(), 1)

    def drain(c):
        store_dk(c).wait()
        store_dv(c).wait()
        for dist in range(1, REACH):

            @pl.when(me + dist < n_ctx)
            def _():
                send_kv(c, dist, 0).wait_send()
                send_kv(c, dist, 1).wait_send()

            @pl.when(me >= dist)
            def _():
                send_part(c, dist).wait_send()

    each(kv_count, drain)
    each(heads, lambda h: (store_out(h).wait(), store_dq(h).wait()))


def local(queries, global_keys, global_values, out_grad, query_gain, doc_start):
    rows = queries.shape[1]
    heads = queries.shape[2] // HD
    kv_count = global_keys.shape[2] // HD
    group = heads // kv_count
    width = REACH * rows
    n_dp = lax.axis_size("dp")
    n_ctx = lax.axis_size("ctx")
    begins = (jnp.repeat(doc_start[0], BLOCK) * BLOCK).reshape(1, rows)
    hbm = pl.BlockSpec(memory_space=pl.ANY)
    vmem = pl.BlockSpec(memory_space=pltpu.VMEM)
    low = jnp.bfloat16
    full = jnp.float32
    dma = pltpu.SemaphoreType.DMA
    attn_out, query_grad, key_grad, value_grad, gain_grad = pl.pallas_call(
        functools.partial(kernel, n_dp, n_ctx),
        out_shape=(
            jax.ShapeDtypeStruct(queries.shape, low),
            jax.ShapeDtypeStruct(queries.shape, low),
            jax.ShapeDtypeStruct(global_keys.shape, low),
            jax.ShapeDtypeStruct(global_keys.shape, low),
            jax.ShapeDtypeStruct((heads, HD), full),
        ),
        in_specs=[hbm, hbm, hbm, hbm, vmem, vmem],
        out_specs=(hbm, hbm, hbm, hbm, vmem),
        scratch_shapes=[
            pltpu.VMEM((heads, rows, HD), low),
            pltpu.VMEM((heads, rows, HD), low),
            pltpu.VMEM((kv_count, 2, REACH, rows, HD), low),
            pltpu.VMEM((rows, rows), full),
            pltpu.VMEM((2, width, rows), full),
            pltpu.VMEM((2, width, rows), full),
            pltpu.VMEM((width, group * rows), low),
            pltpu.VMEM((width, group * rows), low),
            pltpu.VMEM((group * rows, HD), low),
            pltpu.VMEM((HD, width), low),
            pltpu.VMEM((HD, width), low),
            pltpu.VMEM((kv_count, FAR, 2, rows, HD), low),
            pltpu.VMEM((kv_count, FAR, 2, rows, HD), low),
            pltpu.VMEM((kv_count, 2, rows, HD), full),
            pltpu.VMEM((heads, rows, HD), low),
            pltpu.VMEM((heads, rows, HD), low),
            pltpu.VMEM((kv_count, 2, rows, HD), low),
            pltpu.VMEM((heads, HD), full),
            pltpu.VMEM((n_ctx, heads, HD), full),
            pltpu.VMEM((heads, HD), full),
            pltpu.VMEM((n_dp, heads, HD), full),
            dma((2, heads)),
            dma((2, kv_count)),
            dma((kv_count, FAR, 2)),
            dma((kv_count, FAR, 2)),
            dma((kv_count, FAR)),
            dma((kv_count, FAR)),
            dma((2, heads)),
            dma((2, kv_count)),
            dma((n_ctx,)),
            dma((n_ctx,)),
            dma((n_dp,)),
            dma((n_dp,)),
        ],
        compiler_params=pltpu.CompilerParams(
            collective_id=0, has_side_effects=True, vmem_limit_bytes=48 * 1024 * 1024
        ),
    )(queries, global_keys, global_values, out_grad, query_gain.reshape(heads, HD), begins)
    return (attn_out, query_grad, key_grad, value_grad, gain_grad.reshape(-1))


def solution(mesh):
    spec = P("dp", "ctx", None)
    return jax.shard_map(
        local,
        mesh=mesh,
        in_specs=(spec, spec, spec, spec, P(), P("dp", "ctx")),
        out_specs=(spec, spec, spec, spec, P()),
        check_vma=False,
    )
```

time: 235 us -> 89.8 us (0.38)
  Pallas kernels: 0 us -> 80.1 us
  matrix products: 55.5 us -> 0 us
  blocking collectives: 48.4 us -> 0 us
  starting transfers between devices: 40.7 us -> 0 us
  waiting for transfers between devices: 34.7 us -> 0 us
  local copies, waits for them, and re-layouts: 35 us -> 8.11 us
  other arithmetic: 17.3 us -> 0.66 us
    pallas_call x0 -> x1, Pallas kernels: none -> 80.1 us  [local(): pl.pallas_call(functools.partial(kernel, n_dp, n_ctx), out_shape=(jax.Sha...]
    dot_general x24 -> x0, matrix products: 55.5 us -> none  [the longest x4 12.5 us: head_group(): jnp.einsum('gtw,tgd->wd', weights_low, grad_part, preferred_element_type=...]
    psum x1 -> x0, blocking collectives: 48.4 us -> none  [local(): gain_grad = lax.psum(gain_term, ('dp', 'ctx'))]
    ppermute x10 -> x0, starting transfers between devices: 40.7 us -> none  [shifted(): lax.ppermute(value, axis, [(source, source + steps) for source in range(f...]
    ppermute x10 -> x0, waiting for transfers between devices: 34.7 us -> none  [shifted(): lax.ppermute(value, axis, [(source, source + steps) for source in range(f...]
    slice x6 -> x0, local copies, waits for them, and re-layouts: 6.9 us -> none  [the longest x2 3.13 us: local(): key_offsets[:, 1::2]]
    unnamed x41 -> x13, local copies, waits for them, and re-layouts: 14.6 us -> 8.04 us
    transpose x3 -> x0, other arithmetic: 5.11 us -> none  [the longest x1 2.23 us: local(): key_three = window_keys.reshape(width, kv_count, HD).transpose(1, 0, 2)]
  transfers between devices with their start and end apart: 10 -> 0, of which waited for: 2 -> 0; matrix products, arithmetic and copies ran while one was open for 12% -> 0% of each run, Pallas kernels for 0% -> 0%
where the time goes in v1:
time: 89.8 us; the launch traced here: 89.5 us
  Pallas kernels  80.1 us (89%)
  local copies, waits for them, and re-layouts  8.11 us (9%)
    pallas_call x1, Pallas kernels, local(): pl.pallas_call(functools.partial(kernel, n_dp, n_ctx), out_shape=(jax.Sha...  80.1 us
    unnamed x13, local copies, waits for them, and re-layouts  8.04 us

profile of v1, /device:TPU:0, one launch (start us, length us, event | category | flops | bytes accessed | tf_op | source)
XLA Modules:
  0.0 89.5 jit_solution(7419593893090108790)
XLA Ops:
  0.6 0.7 multiply_bitcast_fusion
  1.3 0.1 broadcast_in_dim.3
  1.4 0.0 copy-start
  1.4 1.3 %copy-done = bf16[1,256,2560]{2,1,0:T(8,128)(2,1)S(1)} copy-done((bf16[1,256,2560]{2,1,0:T(8,128)(2,1)S(1)}, bf16[1,256,2560]{2,1,0:T(8,128)(2,1)}, u32[]{:S(2)}) %copy-start) | copy-done | bytes 1310744
  2.7 0.0 copy-start.1
  2.7 0.9 %copy-done.1 = bf16[1,256,512]{2,1,0:T(8,128)(2,1)S(1)} copy-done((bf16[1,256,512]{2,1,0:T(8,128)(2,1)S(1)}, bf16[1,256,512]{2,1,0:T(8,128)(2,1)}, u32[]{:S(2)}) %copy-start.1) | copy-done | bytes 262168
  3.6 0.0 copy-start.2
  3.6 0.9 %copy-done.2 = bf16[1,256,512]{2,1,0:T(8,128)(2,1)S(1)} copy-done((bf16[1,256,512]{2,1,0:T(8,128)(2,1)S(1)}, bf16[1,256,512]{2,1,0:T(8,128)(2,1)}, u32[]{:S(2)}) %copy-start.2) | copy-done | bytes 262168
  4.6 0.0 copy-start.3
  4.6 0.7 copy-done.3
  5.3 80.1 %shard_map.101 = (bf16[1,256,2560]{2,1,0:T(8,128)(2,1)S(1)}, bf16[1,256,2560]{2,1,0:T(8,128)(2,1)S(1)}, bf16[1,256,512]{2,1,0:T(8,128)(2,1)S(1)}, bf16[1,256,512]{2,1,0:T(8,128)(2,1)S(1)}, f32[20,128]{1,0:T(8,128)S(1)}) custom-call(bf16[1,256,2560]{2,1,0:T(8,128)(2,1)S(1)} %copy-done, bf16[1,256,512]{2,1,0:T(8,128)(2,1)S(1)} %copy-done.1, ...), custom_call_target="tpu_custom_call" | custom-call | tf_op jit(solution)/shard_map/pallas_call | solution.py:385
  85.4 1.1 %copy.16 = bf16[1,256,2560]{2,1,0:T(8,128)(2,1)} copy(bf16[1,256,2560]{2,1,0:T(8,128)(2,1)S(1)} %get-tuple-element.20) | data formatting | bytes 2621440
  86.5 1.1 %copy.17 = bf16[1,256,2560]{2,1,0:T(8,128)(2,1)} copy(bf16[1,256,2560]{2,1,0:T(8,128)(2,1)S(1)} %get-tuple-element.21) | data formatting | bytes 2621440
  87.5 0.7 copy.18
  88.2 0.7 copy.19
  88.9 0.6 copy.20
Async XLA Ops:
  1.4 1.3 %copy-start = (bf16[1,256,2560]{2,1,0:T(8,128)(2,1)S(1)}, bf16[1,256,2560]{2,1,0:T(8,128)(2,1)}, u32[]{:S(2)}) copy-start(bf16[1,256,2560]{2,1,0:T(8,128)(2,1)} %q_hbm.1) | copy-start | bytes 3932164
  2.7 0.9 %copy-start.1 = (bf16[1,256,512]{2,1,0:T(8,128)(2,1)S(1)}, bf16[1,256,512]{2,1,0:T(8,128)(2,1)}, u32[]{:S(2)}) copy-start(bf16[1,256,512]{2,1,0:T(8,128)(2,1)} %k_hbm.1) | copy-start | bytes 786436
  3.6 0.9 %copy-start.2 = (bf16[1,256,512]{2,1,0:T(8,128)(2,1)S(1)}, bf16[1,256,512]{2,1,0:T(8,128)(2,1)}, u32[]{:S(2)}) copy-start(bf16[1,256,512]{2,1,0:T(8,128)(2,1)} %v_hbm.1) | copy-start | bytes 786436
  4.6 0.7 copy-start.3

commit v2 on v1

--- a/solution.py
+++ b/solution.py
@@ -91,31 +91,112 @@
         return pltpu.make_async_copy(g_hbm.at[0, :, cols(h)], g_buf.at[h], load_sem.at[1, h])
 
     def load_k(c):
-        return pltpu.make_async_copy(k_hbm.at[0, :, cols(c)], kv_buf.at[c, 0, FAR], own_sem.at[0, c])
+        return pltpu.make_async_copy(k_hbm.at[0, :, cols(c)], kv_buf.at[c, FAR, 0], own_sem.at[0, c])
 
     def load_v(c):
-        return pltpu.make_async_copy(v_hbm.at[0, :, cols(c)], kv_buf.at[c, 1, FAR], own_sem.at[1, c])
-
-    def send_kv(c, dist, which):
-        source = (k_hbm, v_hbm)[which]
+        return pltpu.make_async_copy(v_hbm.at[0, :, cols(c)], kv_buf.at[c, FAR, 1], own_sem.at[1, c])
+
+    odd = lax.rem(me, 2)
+    partner = me + 1 - 2 * odd
+
+    def kv_copy(c, step, source, dist, peer):
         return pltpu.make_async_remote_copy(
-            src_ref=source.at[0, :, cols(c)],
-            dst_ref=kv_buf.at[c, which, FAR - dist],
-            send_sem=send_sem.at[c, dist - 1, which],
-            recv_sem=recv_sem.at[c, dist - 1, which],
-            device_id={"ctx": lax.rem(me + dist, n_ctx)},
+            src_ref=kv_buf.at[c, source],
+            dst_ref=kv_buf.at[c, FAR - dist],
+            send_sem=send_sem.at[c, step],
+            recv_sem=recv_sem.at[c, dist - 1],
+            device_id={"ctx": peer},
             device_id_type=MESH,
         )
 
-    def send_part(c, dist):
+    def cross_kv(c):
+        return kv_copy(c, 0, FAR - 2 * odd, 1, partner)
+
+    def ahead_kv(c):
+        return kv_copy(c, 1, FAR, 2, lax.rem(me + 2, n_ctx))
+
+    def relay_kv(c):
+        return kv_copy(c, 2, FAR - 1, 3, lax.rem(me + 2, n_ctx))
+
+    def wait_kv(c, dist):
+        @pl.when(me >= dist)
+        def _():
+            kv_copy(c, 0, FAR, dist, partner).wait_recv()
+
+    def own_sends(c):
+        load_k(c).wait()
+        load_v(c).wait()
+
+        @pl.when(odd == 0)
+        def _():
+            cross_kv(c).start()
+
+        @pl.when(me + 2 < n_ctx)
+        def _():
+            ahead_kv(c).start()
+
+    def relay_across(c):
+        wait_kv(c, 2)
+
+        @pl.when((odd == 1) & (me >= 2))
+        def _():
+            cross_kv(c).start()
+
+    def relay_ahead(c):
+        wait_kv(c, 1)
+
+        @pl.when((me >= 1) & (me + 2 < n_ctx))
+        def _():
+            relay_kv(c).start()
+
+    def part_copy(c, index, peer):
         return pltpu.make_async_remote_copy(
-            src_ref=part_out.at[c, dist - 1],
-            dst_ref=part_in.at[c, dist - 1],
-            send_sem=psend_sem.at[c, dist - 1],
-            recv_sem=precv_sem.at[c, dist - 1],
-            device_id={"ctx": lax.rem(me + n_ctx - dist, n_ctx)},
+            src_ref=part_out.at[c, index],
+            dst_ref=part_in.at[c, index],
+            send_sem=psend_sem.at[c, index],
+            recv_sem=precv_sem.at[c, index],
+            device_id={"ctx": peer},
             device_id_type=MESH,
         )
+
+    def cross_part(c):
+        return part_copy(c, 0, partner)
+
+    def back_part(c, index):
+        return part_copy(c, index, lax.rem(me + n_ctx - 2, n_ctx))
+
+    def add_part(c, target, source):
+        for which in range(2):
+            both = part_out[c, target, which].astype(jnp.float32) + part_in[
+                c, source, which
+            ].astype(jnp.float32)
+            part_out[c, target, which] = both.astype(jnp.bfloat16)
+
+    def parts_first(c):
+        @pl.when(me >= 3)
+        def _():
+            back_part(c, 2).start()
+
+        @pl.when((odd == 0) & (me >= 2))
+        def _():
+            back_part(c, 1).start()
+
+    def parts_second(c):
+        @pl.when((me >= 1) & (me + 2 < n_ctx))
+        def _():
+            back_part(c, 2).wait_recv()
+            add_part(c, 0, 2)
+
+        @pl.when(me >= 1)
+        def _():
+            cross_part(c).start()
+
+    def parts_third(c):
+        @pl.when((odd == 1) & (me >= 3))
+        def _():
+            cross_part(c).wait_recv()
+            add_part(c, 1, 0)
+            back_part(c, 1).start()
 
     def store_out(h):
         return pltpu.make_async_copy(out_buf.at[h], out_hbm.at[0, :, cols(h)], store_sem.at[0, h])
@@ -202,7 +283,7 @@
 
         @pl.when(me < dist)
         def _():
-            kv_buf[:, :, FAR - dist] = jnp.zeros((kv_count, 2, rows, HD), jnp.bfloat16)
+            kv_buf[:, FAR - dist] = jnp.zeros((kv_count, 2, rows, HD), jnp.bfloat16)
 
     query_pos = me * rows + lax.broadcasted_iota(jnp.int32, (1, rows), 1)
     begins = begins_ref[...]
@@ -211,15 +292,9 @@
 
     pl.semaphore_wait(barrier, n_ctx - 1 + n_dp - 1)
 
-    def start_sends(c):
-        for dist in range(1, REACH):
-
-            @pl.when(me + dist < n_ctx)
-            def _():
-                send_kv(c, dist, 0).start()
-                send_kv(c, dist, 1).start()
-
-    each(kv_count, start_sends)
+    each(min(2, kv_count), own_sends)
+    relay_across(0)
+    relay_ahead(0)
 
     far_blocks = FAR * rows // BLOCK
     shown = []
@@ -227,18 +302,30 @@
         first = (me - FAR) * rows + w * BLOCK
         shown.append(begins <= first)
 
+    def exchange(c, g):
+        @pl.when(c + 1 < kv_count)
+        def _():
+            if g == min(1, group - 1):
+                relay_across(c + 1)
+            if g == min(3, group - 1):
+                relay_ahead(c + 1)
+
+        @pl.when(c >= 1)
+        def _():
+            if g == 0:
+                parts_second(c - 1)
+            if g == min(2, group - 1):
+                parts_third(c - 1)
+
     def one_kv(c):
-        load_k(c).wait()
-        load_v(c).wait()
-        for dist in range(1, REACH):
-
-            @pl.when(me >= dist)
-            def _():
-                send_kv(c, dist, 0).wait_recv()
-                send_kv(c, dist, 1).wait_recv()
-
-        keys = kv_buf[c, 0].reshape(width, HD)
-        values = kv_buf[c, 1].reshape(width, HD)
+        @pl.when(c + 2 < kv_count)
+        def _():
+            own_sends(c + 2)
+
+        wait_kv(c, 3)
+
+        keys = kv_buf[c, :, 0].reshape(width, HD)
+        values = kv_buf[c, :, 1].reshape(width, HD)
         k_t[...] = keys.astype(jnp.float32).T.astype(jnp.bfloat16)
         v_t[...] = values.astype(jnp.float32).T.astype(jnp.bfloat16)
 
@@ -254,8 +341,8 @@
             query = (raw * gain).astype(jnp.bfloat16)
             qs_all[lanes, :] = query
             grad = g_buf[h]
-            s_g[...] = nt(kv_buf[c, 0].reshape(width, HD), query)
-            dp_g[...] = nt(kv_buf[c, 1].reshape(width, HD), grad)
+            s_g[...] = nt(kv_buf[c, :, 0].reshape(width, HD), query)
+            dp_g[...] = nt(kv_buf[c, :, 1].reshape(width, HD), grad)
             near = s_g[FAR * rows :, :] + tri[...]
             s_g[FAR * rows :, :] = near
             top = jnp.max(near, axis=0, keepdims=True)
@@ -288,6 +375,7 @@
             dq_buf[h] = (dscaled * gain).astype(jnp.bfloat16)
             store_dq(h).start()
             term[pl.ds(h, 1), :] = jnp.sum(dscaled * raw, axis=0, keepdims=True)
+            exchange(c, g)
 
         all_grads = g_buf[pl.ds(c * group, group)].reshape(group * rows, HD)
         for dist in range(FAR, -1, -1):
@@ -300,37 +388,35 @@
             else:
                 part_out[c, dist - 1, 0] = dkey.astype(jnp.bfloat16)
                 part_out[c, dist - 1, 1] = dvalue.astype(jnp.bfloat16)
-
-                @pl.when(me >= dist)
-                def _():
-                    send_part(c, dist).start()
+        parts_first(c)
 
     each(kv_count, one_kv)
 
     each(n_ctx, lambda i: send_ctx(i).start(), 1)
 
-    for dist in range(1, REACH):
-
-        @pl.when(me + dist >= n_ctx)
-        def _():
-            part_in[:, dist - 1] = jnp.zeros((kv_count, 2, rows, HD), jnp.bfloat16)
+    last = kv_count - 1
 
     def finish_kv(c):
-        for dist in range(1, REACH):
-
-            @pl.when(me + dist < n_ctx)
-            def _():
-                send_part(c, dist).wait_recv()
+        @pl.when(me + 2 < n_ctx)
+        def _():
+            back_part(c, 1).wait_recv()
+            for which in range(2):
+                part_own[c, which] = part_own[c, which] + part_in[c, 1, which].astype(jnp.float32)
+
+        @pl.when(odd == 0)
+        def _():
+            cross_part(c).wait_recv()
+            for which in range(2):
+                part_own[c, which] = part_own[c, which] + part_in[c, 0, which].astype(jnp.float32)
 
         for which in range(2):
-            whole = part_own[c, which]
-            for dist in range(1, REACH):
-                whole = whole + part_in[c, dist - 1, which].astype(jnp.float32)
-            kv_out[c, which] = whole.astype(jnp.bfloat16)
+            kv_out[c, which] = part_own[c, which].astype(jnp.bfloat16)
         store_dk(c).start()
         store_dv(c).start()
 
-    each(kv_count - 1, finish_kv)
+    parts_second(last)
+    parts_third(last)
+    each(last, finish_kv)
 
     each(n_ctx, lambda i: recv_ctx(lax.rem(me + i, n_ctx)).wait_recv(), 1)
     term_ctx[me] = term[...]
@@ -339,7 +425,7 @@
     )
     each(n_dp, lambda i: send_dp(i).start(), 1)
 
-    finish_kv(kv_count - 1)
+    finish_kv(last)
 
     each(n_dp, lambda i: recv_dp(lax.rem(dp + i, n_dp)).wait_recv(), 1)
     total_dp[dp] = total[...]
@@ -353,19 +439,54 @@
     def drain(c):
         store_dk(c).wait()
         store_dv(c).wait()
-        for dist in range(1, REACH):
-
-            @pl.when(me + dist < n_ctx)
-            def _():
-                send_kv(c, dist, 0).wait_send()
-                send_kv(c, dist, 1).wait_send()
-
-            @pl.when(me >= dist)
-            def _():
-                send_part(c, dist).wait_send()
+
+        @pl.when(me != 1)
+        def _():
+            cross_kv(c).wait_send()
+
+        @pl.when(me + 2 < n_ctx)
+        def _():
+            ahead_kv(c).wait_send()
+
+        @pl.when((me >= 1) & (me + 2 < n_ctx))
+        def _():
+            relay_kv(c).wait_send()
+
+        @pl.when(me >= 1)
+        def _():
+            cross_part(c).wait_send()
+
+        @pl.when(me >= 2)
+        def _():
+            back_part(c, 1).wait_send()
+
+        @pl.when(me >= 3)
+        def _():
+            back_part(c, 2).wait_send()
 
     each(kv_count, drain)
     each(heads, lambda h: (store_out(h).wait(), store_dq(h).wait()))
+
+
+PIECES = 4
+
+
+def hand_on(*refs):
+    count = len(refs) // 2
+    sources, results, sem = refs[:count], refs[count : 2 * count], refs[-1]
+    copies = []
+    for index, (source, result) in enumerate(zip(sources, results)):
+        rows = source.shape[1]
+        pieces = PIECES if rows % (16 * PIECES) == 0 else 1
+        for piece in range(pieces):
+            at = pl.ds(piece * (rows // pieces), rows // pieces)
+            copies.append(
+                pltpu.make_async_copy(source.at[:, at], result.at[:, at], sem.at[index, piece])
+            )
+    for copy in copies:
+        copy.start()
+    for copy in copies:
+        copy.wait()
 
 
 def local(queries, global_keys, global_values, out_grad, query_gain, doc_start):
@@ -382,7 +503,7 @@
     low = jnp.bfloat16
     full = jnp.float32
     dma = pltpu.SemaphoreType.DMA
-    attn_out, query_grad, key_grad, value_grad, gain_grad = pl.pallas_call(
+    *wide, gain_grad = pl.pallas_call(
         functools.partial(kernel, n_dp, n_ctx),
         out_shape=(
             jax.ShapeDtypeStruct(queries.shape, low),
@@ -396,7 +517,7 @@
         scratch_shapes=[
             pltpu.VMEM((heads, rows, HD), low),
             pltpu.VMEM((heads, rows, HD), low),
-            pltpu.VMEM((kv_count, 2, REACH, rows, HD), low),
+            pltpu.VMEM((kv_count, REACH, 2, rows, HD), low),
             pltpu.VMEM((rows, rows), full),
             pltpu.VMEM((2, width, rows), full),
             pltpu.VMEM((2, width, rows), full),
@@ -417,8 +538,8 @@
             pltpu.VMEM((n_dp, heads, HD), full),
             dma((2, heads)),
             dma((2, kv_count)),
-            dma((kv_count, FAR, 2)),
-            dma((kv_count, FAR, 2)),
+            dma((kv_count, FAR)),
+            dma((kv_count, FAR)),
             dma((kv_count, FAR)),
             dma((kv_count, FAR)),
             dma((2, heads)),
@@ -429,9 +550,17 @@
             dma((n_dp,)),
         ],
         compiler_params=pltpu.CompilerParams(
-            collective_id=0, has_side_effects=True, vmem_limit_bytes=48 * 1024 * 1024
+            collective_id=0, has_side_effects=True, vmem_limit_bytes=60 * 1024 * 1024
         ),
     )(queries, global_keys, global_values, out_grad, query_gain.reshape(heads, HD), begins)
+    attn_out, query_grad, key_grad, value_grad = pl.pallas_call(
+        hand_on,
+        out_shape=tuple(jax.ShapeDtypeStruct(item.shape, item.dtype) for item in wide),
+        in_specs=[hbm] * len(wide),
+        out_specs=(hbm,) * len(wide),
+        scratch_shapes=[dma((len(wide), PIECES))],
+        compiler_params=pltpu.CompilerParams(vmem_limit_bytes=60 * 1024 * 1024),
+    )(*wide)
     return (attn_out, query_grad, key_grad, value_grad, gain_grad.reshape(-1))
 
 

time: 89.8 us -> 176 us (1.96)
  Pallas kernels: 80.1 us -> 173 us
  local copies, waits for them, and re-layouts: 8.11 us -> 1.24 us
    pallas_call x0 -> x1, Pallas kernels: none -> 96.5 us  [local(): pl.pallas_call(hand_on, out_shape=tuple((jax.ShapeDtypeStruct(item.shape,...]
    unnamed x13 -> x3, local copies, waits for them, and re-layouts: 8.04 us -> 0.61 us
    pallas_call x1, Pallas kernels: 80.1 us -> 76.9 us  [local(): pl.pallas_call(functools.partial(kernel, n_dp, n_ctx), out_shape=(jax.Sha...]
where the time goes in v2:
time: 176 us
  Pallas kernels  173 us (98%)
    pallas_call x1, Pallas kernels, local(): pl.pallas_call(hand_on, out_shape=tuple((jax.ShapeDtypeStruct(item.shape,...  96.5 us
    pallas_call x1, Pallas kernels, local(): pl.pallas_call(functools.partial(kernel, n_dp, n_ctx), out_shape=(jax.Sha...  76.9 us

profile of v2, /device:TPU:0, one launch (start us, length us, event | category | flops | bytes accessed | tf_op | source)
XLA Modules:
  0.0 176.0 jit_solution(16528772854841897419)
XLA Ops:
  0.6 0.7 multiply_bitcast_fusion
  1.3 0.6 broadcast_in_dim.3
  1.9 76.9 %shard_map.101 = (bf16[1,256,2560]{2,1,0:T(8,128)(2,1)}, bf16[1,256,2560]{2,1,0:T(8,128)(2,1)}, bf16[1,256,512]{2,1,0:T(8,128)(2,1)}, bf16[1,256,512]{2,1,0:T(8,128)(2,1)}, f32[20,128]{1,0:T(8,128)}) custom-call(bf16[1,256,2560]{2,1,0:T(8,128)(2,1)} %q_hbm.1, bf16[1,256,512]{2,1,0:T(8,128)(2,1)} %k_hbm.1, bf16[1,256,512]{2,1,0:T(8,128)(2,1)} %v_hbm.1, ...), custom_call_target="tpu_custom_call" | custom-call | tf_op jit(solution)/shard_map/pallas_call | solution.py:506
  78.8 0.0 copy-start
  78.9 96.5 %shard_map.102 = (bf16[1,256,2560]{2,1,0:T(8,128)(2,1)}, bf16[1,256,2560]{2,1,0:T(8,128)(2,1)}, bf16[1,256,512]{2,1,0:T(8,128)(2,1)}, bf16[1,256,512]{2,1,0:T(8,128)(2,1)}) custom-call(bf16[1,256,2560]{2,1,0:T(8,128)(2,1)} %get-tuple-element.14.refs_0_, bf16[1,256,2560]{2,1,0:T(8,128)(2,1)} %get-tuple-element.15.refs_1_, ...), custom_call_target="tpu_custom_call" | custom-call | tf_op jit(solution)/shard_map/pallas_call | solution.py:556
  175.4 0.0 copy-done
  175.4 0.6 copy.12
Async XLA Ops:
  78.8 96.6 %copy-start = (f32[20,128]{1,0:T(8,128)S(1)}, f32[20,128]{1,0:T(8,128)}, u32[]{:S(2)}) copy-start(f32[20,128]{1,0:T(8,128)} %get-tuple-element.22) | copy-start | bytes 30724

commit v3 on v2

--- a/solution.py
+++ b/solution.py
@@ -32,7 +32,7 @@
     v_hbm,
     g_hbm,
     gain_ref,
-    begins_ref,
+    starts_ref,
     out_hbm,
     dq_hbm,
     dk_hbm,
@@ -286,7 +286,10 @@
             kv_buf[:, FAR - dist] = jnp.zeros((kv_count, 2, rows, HD), jnp.bfloat16)
 
     query_pos = me * rows + lax.broadcasted_iota(jnp.int32, (1, rows), 1)
-    begins = begins_ref[...]
+    lane_block = lax.broadcasted_iota(jnp.int32, (1, rows), 1) // BLOCK
+    begins = jnp.zeros((1, rows), jnp.int32)
+    for b in range(rows // BLOCK):
+        begins = jnp.where(lane_block == b, starts_ref[0, b] * BLOCK, begins)
     key_pos = me * rows + lax.broadcasted_iota(jnp.int32, (rows, rows), 0)
     tri[...] = jnp.where((key_pos <= query_pos) & (key_pos >= begins), 0.0, NEG)
 
@@ -473,20 +476,8 @@
 
 def hand_on(*refs):
     count = len(refs) // 2
-    sources, results, sem = refs[:count], refs[count : 2 * count], refs[-1]
-    copies = []
-    for index, (source, result) in enumerate(zip(sources, results)):
-        rows = source.shape[1]
-        pieces = PIECES if rows % (16 * PIECES) == 0 else 1
-        for piece in range(pieces):
-            at = pl.ds(piece * (rows // pieces), rows // pieces)
-            copies.append(
-                pltpu.make_async_copy(source.at[:, at], result.at[:, at], sem.at[index, piece])
-            )
-    for copy in copies:
-        copy.start()
-    for copy in copies:
-        copy.wait()
+    for source, result in zip(refs[:count], refs[count:]):
+        result[...] = source[...]
 
 
 def local(queries, global_keys, global_values, out_grad, query_gain, doc_start):
@@ -497,7 +488,6 @@
     width = REACH * rows
     n_dp = lax.axis_size("dp")
     n_ctx = lax.axis_size("ctx")
-    begins = (jnp.repeat(doc_start[0], BLOCK) * BLOCK).reshape(1, rows)
     hbm = pl.BlockSpec(memory_space=pl.ANY)
     vmem = pl.BlockSpec(memory_space=pltpu.VMEM)
     low = jnp.bfloat16
@@ -512,7 +502,7 @@
             jax.ShapeDtypeStruct(global_keys.shape, low),
             jax.ShapeDtypeStruct((heads, HD), full),
         ),
-        in_specs=[hbm, hbm, hbm, hbm, vmem, vmem],
+        in_specs=[hbm, hbm, hbm, hbm, vmem, pl.BlockSpec(memory_space=pltpu.SMEM)],
         out_specs=(hbm, hbm, hbm, hbm, vmem),
         scratch_shapes=[
             pltpu.VMEM((heads, rows, HD), low),
@@ -552,13 +542,17 @@
         compiler_params=pltpu.CompilerParams(
             collective_id=0, has_side_effects=True, vmem_limit_bytes=60 * 1024 * 1024
         ),
-    )(queries, global_keys, global_values, out_grad, query_gain.reshape(heads, HD), begins)
+    )(queries, global_keys, global_values, out_grad, query_gain.reshape(heads, HD), doc_start)
+    pieces = PIECES if rows % (16 * PIECES) == 0 else 1
+    blocks = [
+        pl.BlockSpec((1, rows // pieces, item.shape[2]), lambda i: (0, i, 0)) for item in wide
+    ]
     attn_out, query_grad, key_grad, value_grad = pl.pallas_call(
         hand_on,
+        grid=(pieces,),
         out_shape=tuple(jax.ShapeDtypeStruct(item.shape, item.dtype) for item in wide),
-        in_specs=[hbm] * len(wide),
-        out_specs=(hbm,) * len(wide),
-        scratch_shapes=[dma((len(wide), PIECES))],
+        in_specs=blocks,
+        out_specs=tuple(blocks),
         compiler_params=pltpu.CompilerParams(vmem_limit_bytes=60 * 1024 * 1024),
     )(*wide)
     return (attn_out, query_grad, key_grad, value_grad, gain_grad.reshape(-1))

time: 176 us -> 82.6 us (0.47)
  Pallas kernels: 173 us -> 81.1 us
    pallas_call x1, Pallas kernels: 96.5 us -> 4.06 us  [local(): pl.pallas_call(hand_on, grid=(pieces,), out_shape=tuple((jax.ShapeDtypeSt...]
where the time goes in v3:
time: 82.6 us; the launch traced here: 82.4 us
  Pallas kernels  81.1 us (98%)
    pallas_call x1, Pallas kernels, local(): pl.pallas_call(functools.partial(kernel, n_dp, n_ctx), out_shape=(jax.Sha...  77.1 us
    pallas_call x1, Pallas kernels, local(): pl.pallas_call(hand_on, grid=(pieces,), out_shape=tuple((jax.ShapeDtypeSt...  4.06 us

profile of v3, /device:TPU:0, one launch (start us, length us, event | category | flops | bytes accessed | tf_op | source)
XLA Modules:
  0.0 82.4 jit_solution(11155427209126707378)
XLA Ops:
  0.6 77.1 %shard_map.101 = (bf16[1,256,2560]{2,1,0:T(8,128)(2,1)}, bf16[1,256,2560]{2,1,0:T(8,128)(2,1)}, bf16[1,256,512]{2,1,0:T(8,128)(2,1)}, bf16[1,256,512]{2,1,0:T(8,128)(2,1)}, f32[20,128]{1,0:T(8,128)}) custom-call(bf16[1,256,2560]{2,1,0:T(8,128)(2,1)} %q_hbm.1, bf16[1,256,512]{2,1,0:T(8,128)(2,1)} %k_hbm.1, bf16[1,256,512]{2,1,0:T(8,128)(2,1)} %v_hbm.1, ...), custom_call_target="tpu_custom_call" | custom-call | tf_op jit(solution)/shard_map/pallas_call | solution.py:496
  77.7 0.0 copy-start
  77.7 4.1 %shard_map.102 = (bf16[1,256,2560]{2,1,0:T(8,128)(2,1)}, bf16[1,256,2560]{2,1,0:T(8,128)(2,1)}, bf16[1,256,512]{2,1,0:T(8,128)(2,1)}, bf16[1,256,512]{2,1,0:T(8,128)(2,1)}) custom-call(bf16[1,256,2560]{2,1,0:T(8,128)(2,1)} %get-tuple-element.14.refs_0_, bf16[1,256,2560]{2,1,0:T(8,128)(2,1)} %get-tuple-element.15.refs_1_, ...), custom_call_target="tpu_custom_call" | custom-call | tf_op jit(solution)/shard_map/pallas_call | solution.py:550
  81.8 0.0 copy-done
  81.8 0.6 copy.12
Async XLA Ops:
  77.7 4.1 %copy-start = (f32[20,128]{1,0:T(8,128)S(1)}, f32[20,128]{1,0:T(8,128)}, u32[]{:S(2)}) copy-start(f32[20,128]{1,0:T(8,128)} %get-tuple-element.22) | copy-start | bytes 30724
